TPU v7x, 128 devices: a whole 4x4x4 slice. The times are simulated.
128 devices in a mesh: grp: 8 (over x, core), tile: 16 (over y, z).
Axes of the slice: x: 4, y: 4, z: 4, core: 2. Of those that a mesh axis runs over, the one named last changes fastest.
Arguments:
- molecule_coords: float32 [3, 2097152], P(None, ('grp', 'tile')), may hold values from 0 to 1.6
- molecule_speeds: float32 [3, 2097152], P(None, ('grp', 'tile')), may hold values from -6 to 6
- molecule_thermal_state: float32 [2097152], P(('grp', 'tile')), may hold values from 0.5 to 2
- conservative_strength: float32 [2097152], P(('grp', 'tile')), may hold values from 0.05 to 0.5
- noise_keys: int32 [2097152], P(('grp', 'tile')), may hold values from 0 to 32767
- exported_tile_places: int32 [128, 16, 12], P(('grp', 'tile')), may hold values from 0 to 127
- tile_couplings: int32 [128, 1024, 2], P(('grp', 'tile')), may hold values from 0 to 383, as said below
- processor_coupling_tally: int32 [128], P(('grp', 'tile')), may hold values from 512 to 1024
Outputs:
- force_heat: float32 [4, 2097152], P(None, ('grp', 'tile'))
Inputs may be any that keep to these rules, and one draw needn't show every extreme that they name: `tile_couplings`: second slots of workers in the lowest slab are below 192; first slots are below 192.
All inputs are finite; a program needn't handle non-finite values.
Results may differ from a plain program's by a relative error of at most 0.0003.
Values sent between devices are 32-bit elements; how exact they have to be, the bound alone decides.
A program may use at most 128 MiB of HBM per device.

v0:
```python
import math
import jax
import jax.numpy as jnp
from jax import lax
from jax.sharding import PartitionSpec as P

friction = 0.45
noise_amp = 0.3
conductivity = 0.1


def passed_along(value, axis, steps):
    count = lax.axis_size(axis)
    leading, last = (max(0, -steps), min(count, count - steps))
    return lax.ppermute(value, axis, [(source, source + steps) for source in range(leading, last)])


def tile_pair(first, second):
    offset = first[0:3, :, None] - second[0:3, None, :]
    radius = jnp.sqrt(jnp.sum(offset * offset, 0) + 0.01)
    unit = offset / radius
    weight = jnp.maximum(1.0 - radius, 0.0)
    relative = first[3:6, :, None] - second[3:6, None, :]
    along = jnp.sum(unit * relative, 0)
    repulse = 0.5 * (first[7][:, None] + second[7][None, :])
    seed_first = first[8].astype(jnp.int32)
    seed_second = second[8].astype(jnp.int32)
    hashed = (
        seed_first[:, None] * seed_second[None, :] + seed_first[:, None] + seed_second[None, :]
    ) % 65521
    noise = hashed.astype(jnp.float32) * (2.0 / 65521.0) - 1.0
    magnitude = repulse * weight - friction * weight * weight * along + noise_amp * weight * noise
    force = magnitude[None] * unit
    conduct = conductivity * weight * weight * (second[6][None, :] - first[6][:, None])
    viscous = 0.5 * friction * weight * weight * along * along
    on_first = jnp.concatenate([jnp.sum(force, 2), jnp.sum(conduct + viscous, 1)[None]], 0)
    on_second = jnp.concatenate([-jnp.sum(force, 1), jnp.sum(viscous - conduct, 0)[None]], 0)
    return (on_first, on_second)


def tile_self(block_data):
    offset = block_data[0:3, :, None] - block_data[0:3, None, :]
    radius = jnp.sqrt(jnp.sum(offset * offset, 0) + 0.01)
    unit = offset / radius
    weight = jnp.maximum(1.0 - radius, 0.0)
    relative = block_data[3:6, :, None] - block_data[3:6, None, :]
    along = jnp.sum(unit * relative, 0)
    repulse = 0.5 * (block_data[7][:, None] + block_data[7][None, :])
    seed_first = block_data[8].astype(jnp.int32)
    hashed = (
        seed_first[:, None] * seed_first[None, :] + seed_first[:, None] + seed_first[None, :]
    ) % 65521
    noise = hashed.astype(jnp.float32) * (2.0 / 65521.0) - 1.0
    others = 1.0 - jnp.eye(block_data.shape[1], dtype=jnp.float32)
    magnitude = (
        repulse * weight - friction * weight * weight * along + noise_amp * weight * noise
    ) * others
    force = magnitude[None] * unit
    conduct = conductivity * weight * weight * (block_data[6][None, :] - block_data[6][:, None])
    viscous = 0.5 * friction * weight * weight * along * along
    heating = jnp.sum((conduct + viscous) * others, 1)
    return jnp.concatenate([jnp.sum(force, 2), heating[None]], 0)


def one_hot(indices, count):
    return (indices[:, None] == jnp.arange(count, dtype=jnp.int32)[None, :]).astype(jnp.float32)


def per_device(
    molecule_coords,
    molecule_speeds,
    molecule_thermal_state,
    conservative_strength,
    noise_keys,
    exported_tile_places,
    tile_couplings,
    processor_coupling_tally,
):
    n_tile = lax.axis_size("tile")
    blocks = molecule_coords.shape[1] // 128
    slot_table = exported_tile_places[0]
    cap = slot_table.shape[1]
    buffer_len = n_tile * cap
    owned = jnp.concatenate(
        [
            molecule_coords,
            molecule_speeds,
            molecule_thermal_state[None],
            conservative_strength[None],
            noise_keys[None].astype(jnp.float32),
        ],
        0,
    )
    owned = owned.reshape(9, blocks, 128).transpose(1, 0, 2)
    group_data = lax.all_gather(owned, "tile", axis=0, tiled=True)
    tables = lax.all_gather(exported_tile_places, "tile", axis=0, tiled=True)
    my_index = lax.axis_index("tile")
    my_slots = lax.dynamic_index_in_dim(tables, my_index, 1, keepdims=False)
    group_ids = (jnp.arange(n_tile, dtype=jnp.int32)[:, None] * blocks + my_slots).reshape(-1)
    held_blocks = group_data[group_ids]
    neighbour = passed_along(held_blocks, "grp", 1)
    reachable = jnp.concatenate([held_blocks, neighbour], 0)
    total_pair_count = tile_couplings.shape[1]
    batch = math.gcd(total_pair_count, 64)
    first_slots = tile_couplings[0, :, 0].reshape(-1, batch)
    second_slots = tile_couplings[0, :, 1].reshape(-1, batch)
    live_rows = (
        (jnp.arange(total_pair_count, dtype=jnp.int32) < processor_coupling_tally[0])
        .astype(jnp.float32)
        .reshape(-1, batch)
    )

    def consume(carry, items):
        near_acc, far_acc = carry
        first_idx, second_index, live = items
        on_first, on_second = jax.vmap(tile_pair)(held_blocks[first_idx], reachable[second_index])
        on_first = (on_first * live[:, None, None]).reshape(batch, 512)
        on_second = (on_second * live[:, None, None]).reshape(batch, 512)
        near_acc = near_acc + jnp.dot(
            one_hot(first_idx, buffer_len).T, on_first, precision=lax.Precision.HIGHEST
        )
        far_acc = far_acc + jnp.dot(
            one_hot(second_index, 2 * buffer_len).T, on_second, precision=lax.Precision.HIGHEST
        )
        return ((near_acc, far_acc), None)

    start_carry = (
        jnp.zeros((buffer_len, 512), jnp.float32),
        jnp.zeros((2 * buffer_len, 512), jnp.float32),
    )
    (near_acc, far_acc), _ = lax.scan(consume, start_carry, (first_slots, second_slots, live_rows))
    lower_terms = passed_along(far_acc[buffer_len:], "grp", -1)
    own_total = near_acc + far_acc[:buffer_len] + lower_terms
    selector = one_hot(group_ids, n_tile * blocks)
    summed = lax.psum_scatter(
        jnp.dot(selector.T, own_total, precision=lax.Precision.HIGHEST),
        "tile",
        scatter_dimension=0,
        tiled=True,
    )
    self_batch = math.gcd(blocks, 16)

    def self_step(carry, group_data):
        return (carry, jax.vmap(tile_self)(group_data))

    _, selfs = lax.scan(
        self_step, jnp.zeros((), jnp.float32), owned.reshape(-1, self_batch, 9, 128)
    )
    result = summed.reshape(blocks, 4, 128) + selfs.reshape(blocks, 4, 128)
    return result.transpose(1, 0, 2).reshape(4, blocks * 128)


def solution(mesh):
    in_specs = (
        P(None, ("grp", "tile")),
        P(None, ("grp", "tile")),
        P(("grp", "tile")),
        P(("grp", "tile")),
        P(("grp", "tile")),
        P(("grp", "tile"), None, None),
        P(("grp", "tile"), None, None),
        P(("grp", "tile")),
    )
    out_specs = P(None, ("grp", "tile"))
    return jax.shard_map(
        per_device, mesh=mesh, in_specs=in_specs, out_specs=out_specs, check_vma=False
    )
```

profile of v0, /device:TPU:0, one launch (start us, length us, event | category | flops | bytes accessed | tf_op | source)
XLA Modules:
  0.0 833.5 jit_solution(1761941762387604038)
XLA Ops:
  12.7 25.4 %all_gather.6 = s32[16,16,12]{2,1,0:T(8,128)S(1)} all-gather(s32[1,16,12]{2,1,0:T(8,128)S(1)} %copy.32), channel_id=1, replica_groups=mesh['grp'=8,'tile'=16] {'tile'}, dimensions={0}, use_global_device_ids=true | all-gather | bytes 13056 | tf_op jit(solution)/shard_map/all_gather | solution.py:96
  40.1 50.3 %all-gather.2.cloned.1.call-done = f32[2048,9,128]{2,0,1:T(8,128)} async-done(((f32[128,9,128]{2,0,1:T(8,128)}), f32[2048,9,128]{2,0,1:T(8,128)}) %all-gather.2.cloned.1.call-update) | async-done | bytes 9437200 | tf_op jit(solution)/shard_map/all_gather | solution.py:95
  90.5 12.8 %copy.33 = f32[2048,9,128]{2,1,0:T(8,128)} copy(f32[2048,9,128]{2,0,1:T(8,128)} %all-gather.2.cloned.1.call-done) | data formatting | bytes 18874368 | tf_op jit(solution)/shard_map/all_gather | solution.py:95
  117.3 606.1 %while.28 = (s32[]{:T(128)}, f32[192,512]{1,0:T(8,128)}, f32[384,512]{1,0:T(8,128)S(1)}, s32[16,64]{1,0:T(8,128)S(1)}, f32[192,9,128]{2,1,0:T(8,128)S(1)}, /*ind...) while((s32[]{:T(128)}, f32[192,512]{1,0:T(8,128)}, ...), condition=%wide.region_7.8_spmd.clone, body=%wide.region_0.7_spmd.clone.sunk | while | flops 305871232 | bytes 52507452 | solution.py:131
  134.7 9.2 %subtract_reduce_fusion.2 = (f32[64,128]{1,0:T(8,128)S(1)}, f32[64,128]{1,0:T(8,128)S(1)}, f32[64,128,128]{2,1,0:T(8,128)S(1)}) fusion(f32[64,128,128]{2,1,0:T(8,128)S(1)} %multiply_reduce_fusion.11, f32[64,128]{1,0:T(8,128)S(1)} %bitcast.118, f32[64,128]{1,0:T(8,128)S(1)} %bitcast.115, f32[64,128,128]{2,1,0:T(8,128)S(1)} %fusion.72, ...), kind=kLoop, calls=%fused_computation.59.clone.1 | loop fusion | flops 38780928 | bytes 12845056 | tf_op jit(solution)/shard_map/while/body/eval_jaxpr/vmap()/reduce_sum | solution.py:37
  143.9 8.5 %multiply_reduce_fusion.12 = (f32[64,3,128]{2,1,0:T(4,128)S(1)}, f32[64,3,128]{2,1,0:T(4,128)S(1)}) fusion(f32[64,128,128]{2,1,0:T(8,128)S(1)} %get-tuple-element.365, f32[64,128,128]{2,1,0:T(8,128)S(1)} %add_sqrt_fusion.5, f32[64,3,128]{2,1,0:T(4,128)S(1)} %get-tuple-element.356, f32[64,3,128]{2,1,0:T(4,128)S(1)} %get-tuple-element.357), kind=kLoop, calls=%fused_computation.44.clone.1 | loop fusion | flops 15679488 | bytes 8781824 | tf_op jit(solution)/shard_map/while/body/eval_jaxpr/vmap()/reduce_sum | solution.py:37
  172.6 9.2 %subtract_reduce_fusion.2 = (f32[64,128]{1,0:T(8,128)S(1)}, f32[64,128]{1,0:T(8,128)S(1)}, f32[64,128,128]{2,1,0:T(8,128)S(1)}) fusion(f32[64,128,128]{2,1,0:T(8,128)S(1)} %multiply_reduce_fusion.11, f32[64,128]{1,0:T(8,128)S(1)} %bitcast.118, f32[64,128]{1,0:T(8,128)S(1)} %bitcast.115, f32[64,128,128]{2,1,0:T(8,128)S(1)} %fusion.72, ...), kind=kLoop, calls=%fused_computation.59.clone.1 | loop fusion | flops 38780928 | bytes 12845056 | tf_op jit(solution)/shard_map/while/body/eval_jaxpr/vmap()/reduce_sum | solution.py:37
  210.4 9.2 %subtract_reduce_fusion.2 = (f32[64,128]{1,0:T(8,128)S(1)}, f32[64,128]{1,0:T(8,128)S(1)}, f32[64,128,128]{2,1,0:T(8,128)S(1)}) fusion(f32[64,128,128]{2,1,0:T(8,128)S(1)} %multiply_reduce_fusion.11, f32[64,128]{1,0:T(8,128)S(1)} %bitcast.118, f32[64,128]{1,0:T(8,128)S(1)} %bitcast.115, f32[64,128,128]{2,1,0:T(8,128)S(1)} %fusion.72, ...), kind=kLoop, calls=%fused_computation.59.clone.1 | loop fusion | flops 38780928 | bytes 12845056 | tf_op jit(solution)/shard_map/while/body/eval_jaxpr/vmap()/reduce_sum | solution.py:37
  248.3 9.2 %subtract_reduce_fusion.2 = (f32[64,128]{1,0:T(8,128)S(1)}, f32[64,128]{1,0:T(8,128)S(1)}, f32[64,128,128]{2,1,0:T(8,128)S(1)}) fusion(f32[64,128,128]{2,1,0:T(8,128)S(1)} %multiply_reduce_fusion.11, f32[64,128]{1,0:T(8,128)S(1)} %bitcast.118, f32[64,128]{1,0:T(8,128)S(1)} %bitcast.115, f32[64,128,128]{2,1,0:T(8,128)S(1)} %fusion.72, ...), kind=kLoop, calls=%fused_computation.59.clone.1 | loop fusion | flops 38780928 | bytes 12845056 | tf_op jit(solution)/shard_map/while/body/eval_jaxpr/vmap()/reduce_sum | solution.py:37
  286.2 9.2 %subtract_reduce_fusion.2 = (f32[64,128]{1,0:T(8,128)S(1)}, f32[64,128]{1,0:T(8,128)S(1)}, f32[64,128,128]{2,1,0:T(8,128)S(1)}) fusion(f32[64,128,128]{2,1,0:T(8,128)S(1)} %multiply_reduce_fusion.11, f32[64,128]{1,0:T(8,128)S(1)} %bitcast.118, f32[64,128]{1,0:T(8,128)S(1)} %bitcast.115, f32[64,128,128]{2,1,0:T(8,128)S(1)} %fusion.72, ...), kind=kLoop, calls=%fused_computation.59.clone.1 | loop fusion | flops 38780928 | bytes 12845056 | tf_op jit(solution)/shard_map/while/body/eval_jaxpr/vmap()/reduce_sum | solution.py:37
  324.1 9.2 %subtract_reduce_fusion.2 = (f32[64,128]{1,0:T(8,128)S(1)}, f32[64,128]{1,0:T(8,128)S(1)}, f32[64,128,128]{2,1,0:T(8,128)S(1)}) fusion(f32[64,128,128]{2,1,0:T(8,128)S(1)} %multiply_reduce_fusion.11, f32[64,128]{1,0:T(8,128)S(1)} %bitcast.118, f32[64,128]{1,0:T(8,128)S(1)} %bitcast.115, f32[64,128,128]{2,1,0:T(8,128)S(1)} %fusion.72, ...), kind=kLoop, calls=%fused_computation.59.clone.1 | loop fusion | flops 38780928 | bytes 12845056 | tf_op jit(solution)/shard_map/while/body/eval_jaxpr/vmap()/reduce_sum | solution.py:37
  362.0 9.2 %subtract_reduce_fusion.2 = (f32[64,128]{1,0:T(8,128)S(1)}, f32[64,128]{1,0:T(8,128)S(1)}, f32[64,128,128]{2,1,0:T(8,128)S(1)}) fusion(f32[64,128,128]{2,1,0:T(8,128)S(1)} %multiply_reduce_fusion.11, f32[64,128]{1,0:T(8,128)S(1)} %bitcast.118, f32[64,128]{1,0:T(8,128)S(1)} %bitcast.115, f32[64,128,128]{2,1,0:T(8,128)S(1)} %fusion.72, ...), kind=kLoop, calls=%fused_computation.59.clone.1 | loop fusion | flops 38780928 | bytes 12845056 | tf_op jit(solution)/shard_map/while/body/eval_jaxpr/vmap()/reduce_sum | solution.py:37
  399.9 9.2 %subtract_reduce_fusion.2 = (f32[64,128]{1,0:T(8,128)S(1)}, f32[64,128]{1,0:T(8,128)S(1)}, f32[64,128,128]{2,1,0:T(8,128)S(1)}) fusion(f32[64,128,128]{2,1,0:T(8,128)S(1)} %multiply_reduce_fusion.11, f32[64,128]{1,0:T(8,128)S(1)} %bitcast.118, f32[64,128]{1,0:T(8,128)S(1)} %bitcast.115, f32[64,128,128]{2,1,0:T(8,128)S(1)} %fusion.72, ...), kind=kLoop, calls=%fused_computation.59.clone.1 | loop fusion | flops 38780928 | bytes 12845056 | tf_op jit(solution)/shard_map/while/body/eval_jaxpr/vmap()/reduce_sum | solution.py:37
  437.7 9.2 %subtract_reduce_fusion.2 = (f32[64,128]{1,0:T(8,128)S(1)}, f32[64,128]{1,0:T(8,128)S(1)}, f32[64,128,128]{2,1,0:T(8,128)S(1)}) fusion(f32[64,128,128]{2,1,0:T(8,128)S(1)} %multiply_reduce_fusion.11, f32[64,128]{1,0:T(8,128)S(1)} %bitcast.118, f32[64,128]{1,0:T(8,128)S(1)} %bitcast.115, f32[64,128,128]{2,1,0:T(8,128)S(1)} %fusion.72, ...), kind=kLoop, calls=%fused_computation.59.clone.1 | loop fusion | flops 38780928 | bytes 12845056 | tf_op jit(solution)/shard_map/while/body/eval_jaxpr/vmap()/reduce_sum | solution.py:37
  475.6 9.2 %subtract_reduce_fusion.2 = (f32[64,128]{1,0:T(8,128)S(1)}, f32[64,128]{1,0:T(8,128)S(1)}, f32[64,128,128]{2,1,0:T(8,128)S(1)}) fusion(f32[64,128,128]{2,1,0:T(8,128)S(1)} %multiply_reduce_fusion.11, f32[64,128]{1,0:T(8,128)S(1)} %bitcast.118, f32[64,128]{1,0:T(8,128)S(1)} %bitcast.115, f32[64,128,128]{2,1,0:T(8,128)S(1)} %fusion.72, ...), kind=kLoop, calls=%fused_computation.59.clone.1 | loop fusion | flops 38780928 | bytes 12845056 | tf_op jit(solution)/shard_map/while/body/eval_jaxpr/vmap()/reduce_sum | solution.py:37
  513.5 9.2 %subtract_reduce_fusion.2 = (f32[64,128]{1,0:T(8,128)S(1)}, f32[64,128]{1,0:T(8,128)S(1)}, f32[64,128,128]{2,1,0:T(8,128)S(1)}) fusion(f32[64,128,128]{2,1,0:T(8,128)S(1)} %multiply_reduce_fusion.11, f32[64,128]{1,0:T(8,128)S(1)} %bitcast.118, f32[64,128]{1,0:T(8,128)S(1)} %bitcast.115, f32[64,128,128]{2,1,0:T(8,128)S(1)} %fusion.72, ...), kind=kLoop, calls=%fused_computation.59.clone.1 | loop fusion | flops 38780928 | bytes 12845056 | tf_op jit(solution)/shard_map/while/body/eval_jaxpr/vmap()/reduce_sum | solution.py:37
  551.4 9.2 %subtract_reduce_fusion.2 = (f32[64,128]{1,0:T(8,128)S(1)}, f32[64,128]{1,0:T(8,128)S(1)}, f32[64,128,128]{2,1,0:T(8,128)S(1)}) fusion(f32[64,128,128]{2,1,0:T(8,128)S(1)} %multiply_reduce_fusion.11, f32[64,128]{1,0:T(8,128)S(1)} %bitcast.118, f32[64,128]{1,0:T(8,128)S(1)} %bitcast.115, f32[64,128,128]{2,1,0:T(8,128)S(1)} %fusion.72, ...), kind=kLoop, calls=%fused_computation.59.clone.1 | loop fusion | flops 38780928 | bytes 12845056 | tf_op jit(solution)/shard_map/while/body/eval_jaxpr/vmap()/reduce_sum | solution.py:37
  589.2 9.2 %subtract_reduce_fusion.2 = (f32[64,128]{1,0:T(8,128)S(1)}, f32[64,128]{1,0:T(8,128)S(1)}, f32[64,128,128]{2,1,0:T(8,128)S(1)}) fusion(f32[64,128,128]{2,1,0:T(8,128)S(1)} %multiply_reduce_fusion.11, f32[64,128]{1,0:T(8,128)S(1)} %bitcast.118, f32[64,128]{1,0:T(8,128)S(1)} %bitcast.115, f32[64,128,128]{2,1,0:T(8,128)S(1)} %fusion.72, ...), kind=kLoop, calls=%fused_computation.59.clone.1 | loop fusion | flops 38780928 | bytes 12845056 | tf_op jit(solution)/shard_map/while/body/eval_jaxpr/vmap()/reduce_sum | solution.py:37
  627.1 9.2 %subtract_reduce_fusion.2 = (f32[64,128]{1,0:T(8,128)S(1)}, f32[64,128]{1,0:T(8,128)S(1)}, f32[64,128,128]{2,1,0:T(8,128)S(1)}) fusion(f32[64,128,128]{2,1,0:T(8,128)S(1)} %multiply_reduce_fusion.11, f32[64,128]{1,0:T(8,128)S(1)} %bitcast.118, f32[64,128]{1,0:T(8,128)S(1)} %bitcast.115, f32[64,128,128]{2,1,0:T(8,128)S(1)} %fusion.72, ...), kind=kLoop, calls=%fused_computation.59.clone.1 | loop fusion | flops 38780928 | bytes 12845056 | tf_op jit(solution)/shard_map/while/body/eval_jaxpr/vmap()/reduce_sum | solution.py:37
  665.0 9.2 %subtract_reduce_fusion.2 = (f32[64,128]{1,0:T(8,128)S(1)}, f32[64,128]{1,0:T(8,128)S(1)}, f32[64,128,128]{2,1,0:T(8,128)S(1)}) fusion(f32[64,128,128]{2,1,0:T(8,128)S(1)} %multiply_reduce_fusion.11, f32[64,128]{1,0:T(8,128)S(1)} %bitcast.118, f32[64,128]{1,0:T(8,128)S(1)} %bitcast.115, f32[64,128,128]{2,1,0:T(8,128)S(1)} %fusion.72, ...), kind=kLoop, calls=%fused_computation.59.clone.1 | loop fusion | flops 38780928 | bytes 12845056 | tf_op jit(solution)/shard_map/while/body/eval_jaxpr/vmap()/reduce_sum | solution.py:37
  702.9 9.2 %subtract_reduce_fusion.2 = (f32[64,128]{1,0:T(8,128)S(1)}, f32[64,128]{1,0:T(8,128)S(1)}, f32[64,128,128]{2,1,0:T(8,128)S(1)}) fusion(f32[64,128,128]{2,1,0:T(8,128)S(1)} %multiply_reduce_fusion.11, f32[64,128]{1,0:T(8,128)S(1)} %bitcast.118, f32[64,128]{1,0:T(8,128)S(1)} %bitcast.115, f32[64,128,128]{2,1,0:T(8,128)S(1)} %fusion.72, ...), kind=kLoop, calls=%fused_computation.59.clone.1 | loop fusion | flops 38780928 | bytes 12845056 | tf_op jit(solution)/shard_map/while/body/eval_jaxpr/vmap()/reduce_sum | solution.py:37
  725.8 10.5 %collective-permute-done.1 = f32[192,512]{1,0:T(8,128)S(1)} collective-permute-done((f32[192,512]{1,0:T(8,128)S(1)}, f32[192,512]{1,0:T(8,128)S(1)}, u32[]{:S(2)}, u32[]{:S(2)}) %collective-permute-start.1) | collective-permute-done | bytes 393248 | tf_op jit(solution)/shard_map/ppermute | solution.py:15
  741.3 69.2 %while.27 = (s32[]{:T(128)}, f32[8,16,4,128]{3,2,1,0:T(4,128)S(1)}, f32[8,16,9,128]{3,1,0,2:T(8,128)}, s32[]{:T(128)}) while((s32[]{:T(128)}, f32[8,16,4,128]{3,2,1,0:T(4,128)S(1)}, f32[8,16,9,128]{3,1,0,2:T(8,128)}, s32[]{:T(128)}) %tuple.104), condition=%wide.region_14.15_spmd, body=%wide.region_9.14_spmd.sunk | while | flops 18925568 | bytes 11239485 | solution.py:146
  810.5 14.3 %reduce-scatter.2.cloned.1.call-done = f32[128,512]{1,0:T(8,128)} async-done(((f32[2048,512]{1,0:T(8,128)}), f32[128,512]{1,0:T(8,128)}) %reduce-scatter.2.cloned.1.call-update) | async-done | bytes 262160 | tf_op jit(solution)/shard_map/reduce_scatter | solution.py:135
  (682 shorter events, 546.5 us)
Async XLA Ops:
  6.5 83.9 %all-gather.2.cloned.1.call-start = ((), (), s32[]{:S(2)}) async-start(), calls=%async_computation.1 | async-start | bytes 10027008 | tf_op jit(solution)/shard_map/all_gather | solution.py:95
  11.8 813.0 %reduce-scatter.2.cloned.1.call-start = ((), (), s32[]{:S(2)}) async-start(), calls=%async_computation.2 | async-start | bytes 4456448 | tf_op jit(solution)/shard_map/reduce_scatter | solution.py:135
  103.2 9.5 %copy-start.8 = (s32[1,1024,2]{1,2,0:T(2,128)S(1)}, s32[1,1024,2]{1,2,0:T(2,128)}, u32[]{:S(2)}) copy-start(s32[1,1024,2]{1,2,0:T(2,128)} %param.18) | copy-start | bytes 24580
  110.9 4.0 collective-permute-start
  143.9 10.1 %copy-start = (f32[192,512]{1,0:T(8,128)S(1)}, f32[192,512]{1,0:T(8,128)}, u32[]{:S(2)}) copy-start(f32[192,512]{1,0:T(8,128)} %get-tuple-element.382) | copy-start | bytes 1179652 | tf_op jit(solution)/shard_map/while
  181.8 10.1 %copy-start = (f32[192,512]{1,0:T(8,128)S(1)}, f32[192,512]{1,0:T(8,128)}, u32[]{:S(2)}) copy-start(f32[192,512]{1,0:T(8,128)} %get-tuple-element.382) | copy-start | bytes 1179652 | tf_op jit(solution)/shard_map/while
  219.6 10.1 %copy-start = (f32[192,512]{1,0:T(8,128)S(1)}, f32[192,512]{1,0:T(8,128)}, u32[]{:S(2)}) copy-start(f32[192,512]{1,0:T(8,128)} %get-tuple-element.382) | copy-start | bytes 1179652 | tf_op jit(solution)/shard_map/while
  257.5 10.1 %copy-start = (f32[192,512]{1,0:T(8,128)S(1)}, f32[192,512]{1,0:T(8,128)}, u32[]{:S(2)}) copy-start(f32[192,512]{1,0:T(8,128)} %get-tuple-element.382) | copy-start | bytes 1179652 | tf_op jit(solution)/shard_map/while
  295.4 10.1 %copy-start = (f32[192,512]{1,0:T(8,128)S(1)}, f32[192,512]{1,0:T(8,128)}, u32[]{:S(2)}) copy-start(f32[192,512]{1,0:T(8,128)} %get-tuple-element.382) | copy-start | bytes 1179652 | tf_op jit(solution)/shard_map/while
  333.3 8.6 %copy-start.5 = (s32[16,64]{1,0:T(8,128)S(1)}, s32[16,64]{1,0:T(8,128)}, u32[]{:S(2)}) copy-start(s32[16,64]{1,0:T(8,128)} %copy-done.4) | copy-start | bytes 12292 | tf_op jit(solution)/shard_map/while
  333.3 8.6 %copy-start.7 = (s32[16,64]{1,0:T(8,128)S(1)}, s32[16,64]{1,0:T(8,128)}, u32[]{:S(2)}) copy-start(s32[16,64]{1,0:T(8,128)} %copy-done.6) | copy-start | bytes 12292 | tf_op jit(solution)/shard_map/while
  333.3 10.1 %copy-start = (f32[192,512]{1,0:T(8,128)S(1)}, f32[192,512]{1,0:T(8,128)}, u32[]{:S(2)}) copy-start(f32[192,512]{1,0:T(8,128)} %get-tuple-element.382) | copy-start | bytes 1179652 | tf_op jit(solution)/shard_map/while
  371.1 8.6 %copy-start.5 = (s32[16,64]{1,0:T(8,128)S(1)}, s32[16,64]{1,0:T(8,128)}, u32[]{:S(2)}) copy-start(s32[16,64]{1,0:T(8,128)} %copy-done.4) | copy-start | bytes 12292 | tf_op jit(solution)/shard_map/while
  371.2 10.1 %copy-start = (f32[192,512]{1,0:T(8,128)S(1)}, f32[192,512]{1,0:T(8,128)}, u32[]{:S(2)}) copy-start(f32[192,512]{1,0:T(8,128)} %get-tuple-element.382) | copy-start | bytes 1179652 | tf_op jit(solution)/shard_map/while
  409.0 10.1 %copy-start = (f32[192,512]{1,0:T(8,128)S(1)}, f32[192,512]{1,0:T(8,128)}, u32[]{:S(2)}) copy-start(f32[192,512]{1,0:T(8,128)} %get-tuple-element.382) | copy-start | bytes 1179652 | tf_op jit(solution)/shard_map/while
  446.9 10.1 %copy-start = (f32[192,512]{1,0:T(8,128)S(1)}, f32[192,512]{1,0:T(8,128)}, u32[]{:S(2)}) copy-start(f32[192,512]{1,0:T(8,128)} %get-tuple-element.382) | copy-start | bytes 1179652 | tf_op jit(solution)/shard_map/while
  484.8 10.1 %copy-start = (f32[192,512]{1,0:T(8,128)S(1)}, f32[192,512]{1,0:T(8,128)}, u32[]{:S(2)}) copy-start(f32[192,512]{1,0:T(8,128)} %get-tuple-element.382) | copy-start | bytes 1179652 | tf_op jit(solution)/shard_map/while
  522.7 10.1 %copy-start = (f32[192,512]{1,0:T(8,128)S(1)}, f32[192,512]{1,0:T(8,128)}, u32[]{:S(2)}) copy-start(f32[192,512]{1,0:T(8,128)} %get-tuple-element.382) | copy-start | bytes 1179652 | tf_op jit(solution)/shard_map/while
  560.6 10.1 %copy-start = (f32[192,512]{1,0:T(8,128)S(1)}, f32[192,512]{1,0:T(8,128)}, u32[]{:S(2)}) copy-start(f32[192,512]{1,0:T(8,128)} %get-tuple-element.382) | copy-start | bytes 1179652 | tf_op jit(solution)/shard_map/while
  598.4 10.1 %copy-start = (f32[192,512]{1,0:T(8,128)S(1)}, f32[192,512]{1,0:T(8,128)}, u32[]{:S(2)}) copy-start(f32[192,512]{1,0:T(8,128)} %get-tuple-element.382) | copy-start | bytes 1179652 | tf_op jit(solution)/shard_map/while
  636.3 10.1 %copy-start = (f32[192,512]{1,0:T(8,128)S(1)}, f32[192,512]{1,0:T(8,128)}, u32[]{:S(2)}) copy-start(f32[192,512]{1,0:T(8,128)} %get-tuple-element.382) | copy-start | bytes 1179652 | tf_op jit(solution)/shard_map/while
  674.2 10.1 %copy-start = (f32[192,512]{1,0:T(8,128)S(1)}, f32[192,512]{1,0:T(8,128)}, u32[]{:S(2)}) copy-start(f32[192,512]{1,0:T(8,128)} %get-tuple-element.382) | copy-start | bytes 1179652 | tf_op jit(solution)/shard_map/while
  712.1 10.1 %copy-start = (f32[192,512]{1,0:T(8,128)S(1)}, f32[192,512]{1,0:T(8,128)}, u32[]{:S(2)}) copy-start(f32[192,512]{1,0:T(8,128)} %get-tuple-element.382) | copy-start | bytes 1179652 | tf_op jit(solution)/shard_map/while
  723.4 12.9 %collective-permute-start.1 = (f32[192,512]{1,0:T(8,128)S(1)}, f32[192,512]{1,0:T(8,128)S(1)}, u32[]{:S(2)}, u32[]{:S(2)}) collective-permute-start(f32[192,512]{1,0:T(8,128)S(1)} %slice.109), channel_id=1, source_target_pairs={{16,0},{32,16},{48,32},{64,48},{80,64},{96,80},{112,96},{17,1},{33... | collective-permute-start | bytes 1179656 | tf_op jit(solution)/shard_map/ppermute | solution.py:15
  (94 other events, 383.3 us)
Sparse Core Ops, SparseCore 0:
  12.0 78.4 all-gather.1
  741.4 83.3 reduce-scatter.1
where the time goes:
time: 836 us; the launch traced here: 833 us
  other arithmetic  564 us (67%)
  local copies, waits for them, and re-layouts  123 us (15%)
  waiting for transfers between devices  76 us (9%)
  blocking collectives  25.4 us (3%)
  matrix products  23.4 us (3%)
  between operations  14.2 us (2%)
    reduce_sum x16, other arithmetic, tile_pair(): jnp.sum(viscous - conduct, 0)[None]  147 us
    reduce_sum x16, other arithmetic, tile_pair(): jnp.sum(force, 1)  135 us
    reduce_sum x16, other arithmetic, tile_pair(): along = jnp.sum(unit * relative, 0)  128 us
    reduce_sum x16, other arithmetic, tile_pair(): radius = jnp.sqrt(jnp.sum(offset * offset, 0) + 0.01)  66.2 us
    all_gather x1, waiting for transfers between devices, per_device(): group_data = lax.all_gather(owned, 'tile', axis=0, tiled=True)  50.3 us
    gather x16, local copies, waits for them, and re-layouts, consume(): reachable[second_index]  39.7 us
    all_gather x1, blocking collectives, per_device(): tables = lax.all_gather(exported_tile_places, 'tile', axis=0, tiled=True)  25.4 us
    mul x8, other arithmetic, tile_self(): (repulse * weight - friction * weight * weight * along + noise_amp * weig...  19.2 us
  transfers between devices with their start and end apart: 4, of which 4 were waited for; matrix products, arithmetic and copies ran while one was open for 9% of the time, Pallas kernels for 0%

commit v1 on v0

--- a/solution.py
+++ b/solution.py
@@ -93,7 +93,18 @@
     )
     owned = owned.reshape(9, blocks, 128).transpose(1, 0, 2)
     group_data = lax.all_gather(owned, "tile", axis=0, tiled=True)
-    tables = lax.all_gather(exported_tile_places, "tile", axis=0, tiled=True)
+    ways = lax.axis_size("tile")
+    up = [(d, (d + 1) % ways) for d in range(ways)]
+    down = [(d, (d - 1) % ways) for d in range(ways)]
+    earlier, later = ([exported_tile_places], [exported_tile_places])
+    for __2 in range(ways // 2):
+        earlier.append(lax.ppermute(earlier[-1], "tile", up))
+    for __2 in range((ways - 1) // 2):
+        later.append(lax.ppermute(later[-1], "tile", down))
+    line = jnp.concatenate([*earlier[::-1], *later[1:]], axis=0)
+    tables = jnp.roll(
+        line, (lax.axis_index("tile") - ways // 2) * exported_tile_places.shape[0], axis=0
+    )
     my_index = lax.axis_index("tile")
     my_slots = lax.dynamic_index_in_dim(tables, my_index, 1, keepdims=False)
     group_ids = (jnp.arange(n_tile, dtype=jnp.int32)[:, None] * blocks + my_slots).reshape(-1)

time: 836 us -> 835 us (level)
  starting transfers between devices: 3.3 us -> 43.5 us
  blocking collectives: 25.4 us -> 0 us
  waiting for transfers between devices: 76 us -> 61.6 us
    ppermute x0 -> x15, starting transfers between devices: none -> 40 us  [the longest x7 37.9 us: per_device(): later.append(lax.ppermute(later[-1], 'tile', down))]
    all_gather x1, waiting for transfers between devices: 50.3 us -> 19.3 us  [per_device(): group_data = lax.all_gather(owned, 'tile', axis=0, tiled=True)]
    all_gather x1 -> x0, blocking collectives: 25.4 us -> none  [per_device(): tables = lax.all_gather(exported_tile_places, 'tile', axis=0, tiled=True)]
    ppermute x0 -> x15, waiting for transfers between devices: none -> 17.2 us  [the longest x8 17.2 us: per_device(): earlier.append(lax.ppermute(earlier[-1], 'tile', up))]
  transfers between devices with their start and end apart: 4 -> 19, of which waited for: 4 -> 12; matrix products, arithmetic and copies ran while one was open for 9% -> 9% of each run, Pallas kernels for 0% -> 0%
where the time goes in v1:
time: 835 us; the launch traced here: 833 us
  other arithmetic  564 us (68%)
  local copies, waits for them, and re-layouts  122 us (15%)
  waiting for transfers between devices  61.6 us (7%)
  starting transfers between devices  43.5 us (5%)
  matrix products  23.4 us (3%)
  between operations  14.2 us (2%)
    reduce_sum x16, other arithmetic, tile_pair(): jnp.sum(viscous - conduct, 0)[None]  147 us
    reduce_sum x16, other arithmetic, tile_pair(): jnp.sum(force, 1)  135 us
    reduce_sum x16, other arithmetic, tile_pair(): along = jnp.sum(unit * relative, 0)  128 us
    reduce_sum x16, other arithmetic, tile_pair(): radius = jnp.sqrt(jnp.sum(offset * offset, 0) + 0.01)  66.2 us
    gather x16, local copies, waits for them, and re-layouts, consume(): reachable[second_index]  39.7 us
    ppermute x7, starting transfers between devices, per_device(): later.append(lax.ppermute(later[-1], 'tile', down))  37.9 us
    all_gather x1, waiting for transfers between devices, per_device(): group_data = lax.all_gather(owned, 'tile', axis=0, tiled=True)  19.3 us
    mul x8, other arithmetic, tile_self(): (repulse * weight - friction * weight * weight * along + noise_amp * weig...  19.2 us
  transfers between devices with their start and end apart: 19, of which 12 were waited for; matrix products, arithmetic and copies ran while one was open for 9% of the time, Pallas kernels for 0%

profile of v1, /device:TPU:0, one launch (start us, length us, event | category | flops | bytes accessed | tf_op | source)
XLA Modules:
  0.0 833.0 jit_solution(13755779693994445033)
XLA Ops:
  71.5 19.3 %all-gather.2.cloned.1.call-done = f32[2048,9,128]{2,0,1:T(8,128)} async-done(((f32[128,9,128]{2,0,1:T(8,128)}), f32[2048,9,128]{2,0,1:T(8,128)}) %all-gather.2.cloned.1.call-update) | async-done | bytes 9437200 | tf_op jit(solution)/shard_map/all_gather | solution.py:95
  90.7 12.7 %copy.36 = f32[2048,9,128]{2,1,0:T(8,128)} copy(f32[2048,9,128]{2,0,1:T(8,128)} %all-gather.2.cloned.1.call-done) | data formatting | bytes 18874368 | tf_op jit(solution)/shard_map/all_gather | solution.py:95
  117.6 605.7 %while.28 = (s32[]{:T(128)}, f32[192,512]{1,0:T(8,128)}, f32[384,512]{1,0:T(8,128)S(1)}, s32[16,64]{1,0:T(8,128)S(1)}, f32[192,9,128]{2,1,0:T(8,128)S(1)}, /*ind...) while((s32[]{:T(128)}, f32[192,512]{1,0:T(8,128)}, ...), condition=%wide.region_7.8_spmd.clone, body=%wide.region_0.7_spmd.clone.sunk | while | flops 305871232 | bytes 52507452 | solution.py:142
  134.9 9.2 %subtract_reduce_fusion.2 = (f32[64,128]{1,0:T(8,128)S(1)}, f32[64,128]{1,0:T(8,128)S(1)}, f32[64,128,128]{2,1,0:T(8,128)S(1)}) fusion(f32[64,128,128]{2,1,0:T(8,128)S(1)} %multiply_reduce_fusion.11, f32[64,128]{1,0:T(8,128)S(1)} %bitcast.118, f32[64,128]{1,0:T(8,128)S(1)} %bitcast.121, f32[64,128,128]{2,1,0:T(8,128)S(1)} %fusion.71, ...), kind=kLoop, calls=%fused_computation.59.clone.1 | loop fusion | flops 38780928 | bytes 12845056 | tf_op jit(solution)/shard_map/while/body/eval_jaxpr/vmap()/reduce_sum | solution.py:37
  144.1 8.5 %multiply_reduce_fusion.12 = (f32[64,3,128]{2,1,0:T(4,128)S(1)}, f32[64,3,128]{2,1,0:T(4,128)S(1)}) fusion(f32[64,128,128]{2,1,0:T(8,128)S(1)} %get-tuple-element.363, f32[64,128,128]{2,1,0:T(8,128)S(1)} %add_sqrt_fusion.5, f32[64,3,128]{2,1,0:T(4,128)S(1)} %get-tuple-element.354, f32[64,3,128]{2,1,0:T(4,128)S(1)} %get-tuple-element.355), kind=kLoop, calls=%fused_computation.44.clone.1 | loop fusion | flops 15679488 | bytes 8781824 | tf_op jit(solution)/shard_map/while/body/eval_jaxpr/vmap()/reduce_sum | solution.py:37
  172.8 9.2 %subtract_reduce_fusion.2 = (f32[64,128]{1,0:T(8,128)S(1)}, f32[64,128]{1,0:T(8,128)S(1)}, f32[64,128,128]{2,1,0:T(8,128)S(1)}) fusion(f32[64,128,128]{2,1,0:T(8,128)S(1)} %multiply_reduce_fusion.11, f32[64,128]{1,0:T(8,128)S(1)} %bitcast.118, f32[64,128]{1,0:T(8,128)S(1)} %bitcast.121, f32[64,128,128]{2,1,0:T(8,128)S(1)} %fusion.71, ...), kind=kLoop, calls=%fused_computation.59.clone.1 | loop fusion | flops 38780928 | bytes 12845056 | tf_op jit(solution)/shard_map/while/body/eval_jaxpr/vmap()/reduce_sum | solution.py:37
  182.0 8.5 %multiply_reduce_fusion.12 = (f32[64,3,128]{2,1,0:T(4,128)S(1)}, f32[64,3,128]{2,1,0:T(4,128)S(1)}) fusion(f32[64,128,128]{2,1,0:T(8,128)S(1)} %get-tuple-element.363, f32[64,128,128]{2,1,0:T(8,128)S(1)} %add_sqrt_fusion.5, f32[64,3,128]{2,1,0:T(4,128)S(1)} %get-tuple-element.354, f32[64,3,128]{2,1,0:T(4,128)S(1)} %get-tuple-element.355), kind=kLoop, calls=%fused_computation.44.clone.1 | loop fusion | flops 15679488 | bytes 8781824 | tf_op jit(solution)/shard_map/while/body/eval_jaxpr/vmap()/reduce_sum | solution.py:37
  210.6 9.2 %subtract_reduce_fusion.2 = (f32[64,128]{1,0:T(8,128)S(1)}, f32[64,128]{1,0:T(8,128)S(1)}, f32[64,128,128]{2,1,0:T(8,128)S(1)}) fusion(f32[64,128,128]{2,1,0:T(8,128)S(1)} %multiply_reduce_fusion.11, f32[64,128]{1,0:T(8,128)S(1)} %bitcast.118, f32[64,128]{1,0:T(8,128)S(1)} %bitcast.121, f32[64,128,128]{2,1,0:T(8,128)S(1)} %fusion.71, ...), kind=kLoop, calls=%fused_computation.59.clone.1 | loop fusion | flops 38780928 | bytes 12845056 | tf_op jit(solution)/shard_map/while/body/eval_jaxpr/vmap()/reduce_sum | solution.py:37
  248.5 9.2 %subtract_reduce_fusion.2 = (f32[64,128]{1,0:T(8,128)S(1)}, f32[64,128]{1,0:T(8,128)S(1)}, f32[64,128,128]{2,1,0:T(8,128)S(1)}) fusion(f32[64,128,128]{2,1,0:T(8,128)S(1)} %multiply_reduce_fusion.11, f32[64,128]{1,0:T(8,128)S(1)} %bitcast.118, f32[64,128]{1,0:T(8,128)S(1)} %bitcast.121, f32[64,128,128]{2,1,0:T(8,128)S(1)} %fusion.71, ...), kind=kLoop, calls=%fused_computation.59.clone.1 | loop fusion | flops 38780928 | bytes 12845056 | tf_op jit(solution)/shard_map/while/body/eval_jaxpr/vmap()/reduce_sum | solution.py:37
  286.3 9.2 %subtract_reduce_fusion.2 = (f32[64,128]{1,0:T(8,128)S(1)}, f32[64,128]{1,0:T(8,128)S(1)}, f32[64,128,128]{2,1,0:T(8,128)S(1)}) fusion(f32[64,128,128]{2,1,0:T(8,128)S(1)} %multiply_reduce_fusion.11, f32[64,128]{1,0:T(8,128)S(1)} %bitcast.118, f32[64,128]{1,0:T(8,128)S(1)} %bitcast.121, f32[64,128,128]{2,1,0:T(8,128)S(1)} %fusion.71, ...), kind=kLoop, calls=%fused_computation.59.clone.1 | loop fusion | flops 38780928 | bytes 12845056 | tf_op jit(solution)/shard_map/while/body/eval_jaxpr/vmap()/reduce_sum | solution.py:37
  324.2 9.2 %subtract_reduce_fusion.2 = (f32[64,128]{1,0:T(8,128)S(1)}, f32[64,128]{1,0:T(8,128)S(1)}, f32[64,128,128]{2,1,0:T(8,128)S(1)}) fusion(f32[64,128,128]{2,1,0:T(8,128)S(1)} %multiply_reduce_fusion.11, f32[64,128]{1,0:T(8,128)S(1)} %bitcast.118, f32[64,128]{1,0:T(8,128)S(1)} %bitcast.121, f32[64,128,128]{2,1,0:T(8,128)S(1)} %fusion.71, ...), kind=kLoop, calls=%fused_computation.59.clone.1 | loop fusion | flops 38780928 | bytes 12845056 | tf_op jit(solution)/shard_map/while/body/eval_jaxpr/vmap()/reduce_sum | solution.py:37
  362.0 9.2 %subtract_reduce_fusion.2 = (f32[64,128]{1,0:T(8,128)S(1)}, f32[64,128]{1,0:T(8,128)S(1)}, f32[64,128,128]{2,1,0:T(8,128)S(1)}) fusion(f32[64,128,128]{2,1,0:T(8,128)S(1)} %multiply_reduce_fusion.11, f32[64,128]{1,0:T(8,128)S(1)} %bitcast.118, f32[64,128]{1,0:T(8,128)S(1)} %bitcast.121, f32[64,128,128]{2,1,0:T(8,128)S(1)} %fusion.71, ...), kind=kLoop, calls=%fused_computation.59.clone.1 | loop fusion | flops 38780928 | bytes 12845056 | tf_op jit(solution)/shard_map/while/body/eval_jaxpr/vmap()/reduce_sum | solution.py:37
  399.9 9.2 %subtract_reduce_fusion.2 = (f32[64,128]{1,0:T(8,128)S(1)}, f32[64,128]{1,0:T(8,128)S(1)}, f32[64,128,128]{2,1,0:T(8,128)S(1)}) fusion(f32[64,128,128]{2,1,0:T(8,128)S(1)} %multiply_reduce_fusion.11, f32[64,128]{1,0:T(8,128)S(1)} %bitcast.118, f32[64,128]{1,0:T(8,128)S(1)} %bitcast.121, f32[64,128,128]{2,1,0:T(8,128)S(1)} %fusion.71, ...), kind=kLoop, calls=%fused_computation.59.clone.1 | loop fusion | flops 38780928 | bytes 12845056 | tf_op jit(solution)/shard_map/while/body/eval_jaxpr/vmap()/reduce_sum | solution.py:37
  437.7 9.2 %subtract_reduce_fusion.2 = (f32[64,128]{1,0:T(8,128)S(1)}, f32[64,128]{1,0:T(8,128)S(1)}, f32[64,128,128]{2,1,0:T(8,128)S(1)}) fusion(f32[64,128,128]{2,1,0:T(8,128)S(1)} %multiply_reduce_fusion.11, f32[64,128]{1,0:T(8,128)S(1)} %bitcast.118, f32[64,128]{1,0:T(8,128)S(1)} %bitcast.121, f32[64,128,128]{2,1,0:T(8,128)S(1)} %fusion.71, ...), kind=kLoop, calls=%fused_computation.59.clone.1 | loop fusion | flops 38780928 | bytes 12845056 | tf_op jit(solution)/shard_map/while/body/eval_jaxpr/vmap()/reduce_sum | solution.py:37
  475.6 9.2 %subtract_reduce_fusion.2 = (f32[64,128]{1,0:T(8,128)S(1)}, f32[64,128]{1,0:T(8,128)S(1)}, f32[64,128,128]{2,1,0:T(8,128)S(1)}) fusion(f32[64,128,128]{2,1,0:T(8,128)S(1)} %multiply_reduce_fusion.11, f32[64,128]{1,0:T(8,128)S(1)} %bitcast.118, f32[64,128]{1,0:T(8,128)S(1)} %bitcast.121, f32[64,128,128]{2,1,0:T(8,128)S(1)} %fusion.71, ...), kind=kLoop, calls=%fused_computation.59.clone.1 | loop fusion | flops 38780928 | bytes 12845056 | tf_op jit(solution)/shard_map/while/body/eval_jaxpr/vmap()/reduce_sum | solution.py:37
  513.4 9.2 %subtract_reduce_fusion.2 = (f32[64,128]{1,0:T(8,128)S(1)}, f32[64,128]{1,0:T(8,128)S(1)}, f32[64,128,128]{2,1,0:T(8,128)S(1)}) fusion(f32[64,128,128]{2,1,0:T(8,128)S(1)} %multiply_reduce_fusion.11, f32[64,128]{1,0:T(8,128)S(1)} %bitcast.118, f32[64,128]{1,0:T(8,128)S(1)} %bitcast.121, f32[64,128,128]{2,1,0:T(8,128)S(1)} %fusion.71, ...), kind=kLoop, calls=%fused_computation.59.clone.1 | loop fusion | flops 38780928 | bytes 12845056 | tf_op jit(solution)/shard_map/while/body/eval_jaxpr/vmap()/reduce_sum | solution.py:37
  551.3 9.2 %subtract_reduce_fusion.2 = (f32[64,128]{1,0:T(8,128)S(1)}, f32[64,128]{1,0:T(8,128)S(1)}, f32[64,128,128]{2,1,0:T(8,128)S(1)}) fusion(f32[64,128,128]{2,1,0:T(8,128)S(1)} %multiply_reduce_fusion.11, f32[64,128]{1,0:T(8,128)S(1)} %bitcast.118, f32[64,128]{1,0:T(8,128)S(1)} %bitcast.121, f32[64,128,128]{2,1,0:T(8,128)S(1)} %fusion.71, ...), kind=kLoop, calls=%fused_computation.59.clone.1 | loop fusion | flops 38780928 | bytes 12845056 | tf_op jit(solution)/shard_map/while/body/eval_jaxpr/vmap()/reduce_sum | solution.py:37
  589.2 9.2 %subtract_reduce_fusion.2 = (f32[64,128]{1,0:T(8,128)S(1)}, f32[64,128]{1,0:T(8,128)S(1)}, f32[64,128,128]{2,1,0:T(8,128)S(1)}) fusion(f32[64,128,128]{2,1,0:T(8,128)S(1)} %multiply_reduce_fusion.11, f32[64,128]{1,0:T(8,128)S(1)} %bitcast.118, f32[64,128]{1,0:T(8,128)S(1)} %bitcast.121, f32[64,128,128]{2,1,0:T(8,128)S(1)} %fusion.71, ...), kind=kLoop, calls=%fused_computation.59.clone.1 | loop fusion | flops 38780928 | bytes 12845056 | tf_op jit(solution)/shard_map/while/body/eval_jaxpr/vmap()/reduce_sum | solution.py:37
  627.0 9.2 %subtract_reduce_fusion.2 = (f32[64,128]{1,0:T(8,128)S(1)}, f32[64,128]{1,0:T(8,128)S(1)}, f32[64,128,128]{2,1,0:T(8,128)S(1)}) fusion(f32[64,128,128]{2,1,0:T(8,128)S(1)} %multiply_reduce_fusion.11, f32[64,128]{1,0:T(8,128)S(1)} %bitcast.118, f32[64,128]{1,0:T(8,128)S(1)} %bitcast.121, f32[64,128,128]{2,1,0:T(8,128)S(1)} %fusion.71, ...), kind=kLoop, calls=%fused_computation.59.clone.1 | loop fusion | flops 38780928 | bytes 12845056 | tf_op jit(solution)/shard_map/while/body/eval_jaxpr/vmap()/reduce_sum | solution.py:37
  664.9 9.2 %subtract_reduce_fusion.2 = (f32[64,128]{1,0:T(8,128)S(1)}, f32[64,128]{1,0:T(8,128)S(1)}, f32[64,128,128]{2,1,0:T(8,128)S(1)}) fusion(f32[64,128,128]{2,1,0:T(8,128)S(1)} %multiply_reduce_fusion.11, f32[64,128]{1,0:T(8,128)S(1)} %bitcast.118, f32[64,128]{1,0:T(8,128)S(1)} %bitcast.121, f32[64,128,128]{2,1,0:T(8,128)S(1)} %fusion.71, ...), kind=kLoop, calls=%fused_computation.59.clone.1 | loop fusion | flops 38780928 | bytes 12845056 | tf_op jit(solution)/shard_map/while/body/eval_jaxpr/vmap()/reduce_sum | solution.py:37
  702.7 9.2 %subtract_reduce_fusion.2 = (f32[64,128]{1,0:T(8,128)S(1)}, f32[64,128]{1,0:T(8,128)S(1)}, f32[64,128,128]{2,1,0:T(8,128)S(1)}) fusion(f32[64,128,128]{2,1,0:T(8,128)S(1)} %multiply_reduce_fusion.11, f32[64,128]{1,0:T(8,128)S(1)} %bitcast.118, f32[64,128]{1,0:T(8,128)S(1)} %bitcast.121, f32[64,128,128]{2,1,0:T(8,128)S(1)} %fusion.71, ...), kind=kLoop, calls=%fused_computation.59.clone.1 | loop fusion | flops 38780928 | bytes 12845056 | tf_op jit(solution)/shard_map/while/body/eval_jaxpr/vmap()/reduce_sum | solution.py:37
  725.7 10.5 %collective-permute-done.16 = f32[192,512]{1,0:T(8,128)S(1)} collective-permute-done((f32[192,512]{1,0:T(8,128)S(1)}, f32[192,512]{1,0:T(8,128)S(1)}, u32[]{:S(2)}, u32[]{:S(2)}) %collective-permute-start.16) | collective-permute-done | bytes 393248 | tf_op jit(solution)/shard_map/ppermute | solution.py:15
  741.1 69.2 %while.27 = (s32[]{:T(128)}, f32[8,16,4,128]{3,2,1,0:T(4,128)S(1)}, f32[8,16,9,128]{3,1,0,2:T(8,128)}, s32[]{:T(128)}) while((s32[]{:T(128)}, f32[8,16,4,128]{3,2,1,0:T(4,128)S(1)}, f32[8,16,9,128]{3,1,0,2:T(8,128)}, s32[]{:T(128)}) %tuple.103), condition=%wide.region_14.15_spmd, body=%wide.region_9.14_spmd.sunk | while | flops 18925568 | bytes 11239485 | solution.py:157
  810.4 14.0 %reduce-scatter.2.cloned.1.call-done = f32[128,512]{1,0:T(8,128)} async-done(((f32[2048,512]{1,0:T(8,128)}), f32[128,512]{1,0:T(8,128)}) %reduce-scatter.2.cloned.1.call-update) | async-done | bytes 262160 | tf_op jit(solution)/shard_map/reduce_scatter | solution.py:146
  (713 shorter events, 594.4 us)
Async XLA Ops:
  6.5 84.2 %all-gather.2.cloned.1.call-start = ((), (), s32[]{:S(2)}) async-start(), calls=%async_computation.1 | async-start | bytes 10027008 | tf_op jit(solution)/shard_map/all_gather | solution.py:95
  11.9 812.5 %reduce-scatter.2.cloned.1.call-start = ((), (), s32[]{:S(2)}) async-start(), calls=%async_computation.2 | async-start | bytes 4456448 | tf_op jit(solution)/shard_map/reduce_scatter | solution.py:146
  11.9 8.5 %collective-permute-start = (s32[1,16,12]{1,0,2:T(1,128)}, s32[1,16,12]{1,0,2:T(1,128)S(1)}, u32[]{:S(2)}, u32[]{:S(2)}) collective-permute-start(s32[1,16,12]{1,0,2:T(1,128)} %param.17), channel_id=1, source_target_pairs={{0,1},{1,2},{2,3},{3,4},{4,5},{5,6},{6,7},{7,8},{8,9},{9,10},{10,1... | collective-permute-start | bytes 2312 | tf_op jit(solution)/shard_map/ppermute | solution.py:101
  14.0 6.4 collective-permute-start.8
  20.4 6.9 collective-permute-start.1
  20.4 6.9 collective-permute-start.9
  27.3 7.0 collective-permute-start.2
  27.3 7.0 collective-permute-start.10
  34.4 6.9 collective-permute-start.3
  34.4 6.9 collective-permute-start.11
  41.3 6.9 collective-permute-start.4
  41.3 7.0 collective-permute-start.12
  48.3 7.0 collective-permute-start.5
  48.3 7.0 collective-permute-start.13
  55.2 7.1 collective-permute-start.6
  55.2 7.2 collective-permute-start.14
  62.3 7.1 collective-permute-start.7
  71.3 32.1 %copy-start.4 = (s32[16,1,12]{2,0,1:T(8,128)}, s32[16,1,12]{2,0,1:T(8,128)S(1)}, u32[]{:S(2)}) copy-start(s32[16,1,12]{2,0,1:T(8,128)S(1)} %copy.34) | copy-start | bytes 2308
  111.2 4.0 collective-permute-start.15
  446.9 10.1 %copy-start = (f32[192,512]{1,0:T(8,128)S(1)}, f32[192,512]{1,0:T(8,128)}, u32[]{:S(2)}) copy-start(f32[192,512]{1,0:T(8,128)} %get-tuple-element.380) | copy-start | bytes 1179652 | tf_op jit(solution)/shard_map/while
  484.8 10.1 %copy-start = (f32[192,512]{1,0:T(8,128)S(1)}, f32[192,512]{1,0:T(8,128)}, u32[]{:S(2)}) copy-start(f32[192,512]{1,0:T(8,128)} %get-tuple-element.380) | copy-start | bytes 1179652 | tf_op jit(solution)/shard_map/while
  522.6 10.1 %copy-start = (f32[192,512]{1,0:T(8,128)S(1)}, f32[192,512]{1,0:T(8,128)}, u32[]{:S(2)}) copy-start(f32[192,512]{1,0:T(8,128)} %get-tuple-element.380) | copy-start | bytes 1179652 | tf_op jit(solution)/shard_map/while
  636.2 10.1 %copy-start = (f32[192,512]{1,0:T(8,128)S(1)}, f32[192,512]{1,0:T(8,128)}, u32[]{:S(2)}) copy-start(f32[192,512]{1,0:T(8,128)} %get-tuple-element.380) | copy-start | bytes 1179652 | tf_op jit(solution)/shard_map/while
  723.3 12.9 %collective-permute-start.16 = (f32[192,512]{1,0:T(8,128)S(1)}, f32[192,512]{1,0:T(8,128)S(1)}, u32[]{:S(2)}, u32[]{:S(2)}) collective-permute-start(f32[192,512]{1,0:T(8,128)S(1)} %slice.109), channel_id=1, source_target_pairs={{16,0},{32,16},{48,32},{64,48},{80,64},{96,80},{112,96},{17,1},{33... | collective-permute-start | bytes 1179656 | tf_op jit(solution)/shard_map/ppermute | solution.py:15
  (110 other events, 539.6 us)
Sparse Core Ops, SparseCore 0:
  12.0 78.6 all-gather.1
  741.3 83.0 reduce-scatter.1
